TPU v7x, 512 devices: a whole 4x4x16 slice. The times are simulated.
512 devices in a mesh: slab: 64 (over z, x_lo, core), mode: 8 (over x_hi, y).
Axes of the slice: x: 4 (x_hi: 2, x_lo: 2; x = x_hi * 2 + x_lo), y: 4, z: 16, core: 2. Of those that a mesh axis runs over, the one named last changes fastest.
Arguments:
- initial_block: bfloat16 [96, 64, 64, 128], P('mode', 'slab'), may hold values from -180 to 180
- labels: int32 [64, 64, 128], P('slab'), may hold values from 0 to 3
- filter_low: float32 [], replicated, may hold values from 1 to 3
- filter_high: float32 [], replicated, may hold values from 22 to 24
Outputs:
- modes_out: bfloat16 [96, 64, 64, 128], P('mode', 'slab')
- projected: float32 [96, 96], replicated
Inputs may be any that keep to these rules, and one draw needn't show every extreme that they name: `labels`: 0 marks a voxel outside the brain; 1, 2 and 3 are tissue classes.
All inputs are finite; a program needn't handle non-finite values.
Results may differ from a plain program's by a relative error of at most 0.0015.
The roundings to bfloat16 on the way count: a program that leaves them out, or rounds other values in their place, can miss the bound.
Values may be sent and summed in bfloat16 or wider, within the bound.
No kernel may reach another device: no remote copies, remote signals or barrier semaphores. Data moves between devices by JAX's collectives and lax.ppermute only.
A program may use at most 64 MiB of HBM per device.

v0:
```python
import math
import jax
import jax.numpy as jnp
from jax import lax
from jax.sharding import PartitionSpec as P

DEGREE = 4
ROOTS = (0.0, 0.7745967, 1.0, 1.3416408)


def padded_2(shard, sides, width):
    for axis, dim in sides:
        peers, length = (lax.axis_size(axis), shard.shape[dim])
        up = [(i, (i + 1) % peers) for i in range(peers - 1)]
        down = [(j, i) for i, j in up]
        last = lax.slice_in_dim(shard, length - width, length, axis=dim)
        first = lax.slice_in_dim(shard, 0, width, axis=dim)
        before = lax.ppermute(last, axis, up)
        after = lax.ppermute(first, axis, down)
        shard = jnp.concatenate([before, shard, after], axis=dim)
    return shard


def strength_of(labels):
    total = jnp.zeros(labels.shape, jnp.float32)
    for level in range(1, 4):
        total = total + jnp.where(labels == level, ROOTS[level], 0.0)
    return total


def face_weights(strong, padded):
    return (
        strong * padded[:-2, 1:-1, 1:-1],
        strong * padded[2:, 1:-1, 1:-1],
        strong * padded[1:-1, :-2, 1:-1],
        strong * padded[1:-1, 2:, 1:-1],
        strong * padded[1:-1, 1:-1, :-2],
        strong * padded[1:-1, 1:-1, 2:],
    )


def combine_faces(field, padded, weights):
    beside_all = (
        padded[:, :-2, 1:-1, 1:-1],
        padded[:, 2:, 1:-1, 1:-1],
        padded[:, 1:-1, :-2, 1:-1],
        padded[:, 1:-1, 2:, 1:-1],
        padded[:, 1:-1, 1:-1, :-2],
        padded[:, 1:-1, 1:-1, 2:],
    )
    total = weights[0] * (field - beside_all[0])
    for weight, other in zip(weights[1:], beside_all[1:]):
        total = total + weight * (field - other)
    return total


def chebyshev(block, apply_fn, low, high):
    centre = 0.5 * (high + low)
    half = 0.5 * (high - low)
    prev = block
    cur = (apply_fn(block) - centre * block) / half
    for step in range(DEGREE - 1):
        nxt = 2.0 * (apply_fn(cur) - centre * cur) / half - prev
        prev, cur = (cur, nxt)
    return cur


def factor(gram, cross):
    lower = jnp.linalg.cholesky(gram)
    inverse = jax.scipy.linalg.solve_triangular(
        lower, jnp.eye(gram.shape[0], dtype=jnp.float32), lower=True
    )
    projected = jnp.dot(
        jnp.dot(inverse, cross, precision=lax.Precision.HIGHEST),
        inverse.T,
        precision=lax.Precision.HIGHEST,
    )
    return (projected, inverse.T.astype(jnp.bfloat16))


def per_device(initial_block, labels, filter_low, filter_high):
    local = initial_block.shape[0]
    modes = local * lax.axis_size("mode")
    depth, height, width = labels.shape
    scale = math.sqrt(depth * height * width * lax.axis_size("slab"))
    strong = strength_of(labels)
    mask = (labels > 0).astype(jnp.float32)
    rim = padded_2(strong, (("slab", 0),), 1)
    weights = face_weights(strong, jnp.pad(rim, ((0, 0), (1, 1), (1, 1))))

    def apply_fn(field):
        padded = padded_2(field, (("slab", 1),), 1)
        return combine_faces(field, jnp.pad(padded, ((0, 0), (0, 0), (1, 1), (1, 1))), weights)

    block = initial_block.astype(jnp.float32) * mask[None]
    cur = chebyshev(block, apply_fn, filter_low, filter_high)
    filtered = cur.astype(jnp.bfloat16)
    applied = apply_fn(cur).astype(jnp.bfloat16)
    everything = lax.all_gather(filtered, "mode", axis=0, tiled=True)
    whole = everything.reshape(modes, -1)
    own = filtered.reshape(local, -1)
    own_applied = applied.reshape(local, -1)
    gram_block = jnp.einsum("mc,nc->mn", whole, own, preferred_element_type=jnp.float32)
    cross_block = jnp.einsum("mc,nc->mn", whole, own_applied, preferred_element_type=jnp.float32)
    gram_sum, cross_sum = lax.psum((gram_block, cross_block), "slab")
    gram, cross = (
        lax.all_gather(gram_sum, "mode", axis=1, tiled=True),
        lax.all_gather(cross_sum, "mode", axis=1, tiled=True),
    )
    projected, rotation = factor(gram, cross)
    columns = lax.dynamic_slice_in_dim(rotation, lax.axis_index("mode") * local, local, 1)
    turned = jnp.einsum("mj,mc->jc", columns, whole, preferred_element_type=jnp.float32)
    modes_out = (turned * scale).astype(jnp.bfloat16).reshape(local, depth, height, width)
    return (modes_out, projected)


def solution(mesh):
    placed = (P("mode", "slab", None, None), P("slab", None, None), P(), P())
    return jax.shard_map(
        per_device,
        mesh=mesh,
        in_specs=placed,
        out_specs=(P("mode", "slab", None, None), P()),
        check_vma=False,
    )
```

profile of v0, /device:TPU:4, one launch (start us, length us, event | category | flops | bytes accessed | tf_op | source)
XLA Modules:
  0.0 454.6 jit_solution(9304281027527931800)
XLA Ops:
  7.2 0.0 all-gather.4.cloned.1.call-start
  7.2 0.8 convert_bitcast_fusion
  8.0 0.0 copy-start
  8.0 1.0 convert_multiply_fusion
  9.0 1.8 collective-permute-start.1
  10.8 1.3 collective-permute-start.3
  12.1 0.8 select_add_fusion
  12.9 4.0 collective-permute-start
  16.9 1.3 collective-permute-start.2
  19.5 0.0 collective-permute-done
  19.5 1.7 collective-permute-done.2
  21.2 0.1 select_maximum_fusion.10
  21.3 0.9 multiply_bitcast_fusion.1
  22.2 0.0 collective-permute-done.1
  22.2 0.0 collective-permute-done.3
  22.2 0.8 select_maximum_fusion.8
  23.0 0.0 copy-done
  23.0 0.5 fusion.66
  23.5 4.6 %collective-permute-start.4 = (f32[12,1,64,128]{3,2,1,0:T(8,128)S(1)}, f32[12,1,64,128]{3,2,1,0:T(8,128)S(1)}, u32[]{:S(2)}, u32[]{:S(2)}) collective-permute-start(f32[12,1,64,128]{3,2,1,0:T(8,128)S(1)} %fusion.66), channel_id=1, source_target_pairs={{0,8},{8,16},{16,24},{24,32},{32,40},{40,48},{48,56},{56,64},{64,7... | collective-permute-start | bytes 1179656 | tf_op jit(solution)/shard_map/ppermute | solution.py:18
  28.1 1.3 collective-permute-start.5
  29.4 0.0 collective-permute-done.4
  29.4 3.0 collective-permute-done.5
  32.4 0.8 select_maximum_fusion.6
  33.2 0.5 fusion.56
  33.7 9.0 %collective-permute-start.6 = (f32[12,1,64,128]{3,2,1,0:T(8,128)S(1)}, f32[12,1,64,128]{3,2,1,0:T(8,128)S(1)}, u32[]{:S(2)}, u32[]{:S(2)}) collective-permute-start(f32[12,1,64,128]{3,2,1,0:T(8,128)S(1)} %fusion.56), channel_id=1, source_target_pairs={{0,8},{8,16},{16,24},{24,32},{32,40},{40,48},{48,56},{56,64},{64,7... | collective-permute-start | bytes 1179656 | tf_op jit(solution)/shard_map/ppermute | solution.py:18
  42.7 1.3 collective-permute-start.7
  44.0 0.0 collective-permute-done.6
  44.0 2.3 collective-permute-done.7
  46.3 0.8 select_maximum_fusion.4
  47.1 0.5 fusion.44
  47.6 8.3 %collective-permute-start.8 = (f32[12,1,64,128]{3,2,1,0:T(8,128)S(1)}, f32[12,1,64,128]{3,2,1,0:T(8,128)S(1)}, u32[]{:S(2)}, u32[]{:S(2)}) collective-permute-start(f32[12,1,64,128]{3,2,1,0:T(8,128)S(1)} %fusion.44), channel_id=1, source_target_pairs={{0,8},{8,16},{16,24},{24,32},{32,40},{40,48},{48,56},{56,64},{64,7... | collective-permute-start | bytes 1179656 | tf_op jit(solution)/shard_map/ppermute | solution.py:18
  55.9 1.3 collective-permute-start.9
  57.2 0.0 collective-permute-done.8
  57.2 2.3 collective-permute-done.9
  59.5 0.8 select_maximum_fusion.2
  60.3 1.2 fusion.88
  61.5 0.0 all-gather.4.cloned.1.call-update
  61.5 8.3 %collective-permute-start.10 = (f32[12,1,64,128]{3,2,1,0:T(8,128)S(1)}, f32[12,1,64,128]{3,2,1,0:T(8,128)S(1)}, u32[]{:S(2)}, u32[]{:S(2)}) collective-permute-start(f32[12,1,64,128]{3,2,1,0:T(8,128)S(1)} %get-tuple-element.11), channel_id=1, source_target_pairs={{0,8},{8,16},{16,24},{24,32},{32,40},{40,48},{48,56},{56,64},{64,7... | collective-permute-start | bytes 1179656 | tf_op jit(solution)/shard_map/ppermute | solution.py:18
  69.8 1.3 collective-permute-start.11
  71.1 0.0 collective-permute-done.10
  71.1 2.3 collective-permute-done.11
  73.4 0.8 select_maximum_fusion
  74.2 0.0 copy-start.2
  74.2 0.5 fusion.78
  74.7 67.0 %all-gather.4.cloned.1.call-done = bf16[96,1,64,128]{3,2,1,0:T(8,128)(2,1)} async-done(((bf16[12,1,64,128]{3,2,1,0:T(8,128)(2,1)}), bf16[96,1,64,128]{3,2,1,0:T(8,128)(2,1)}) %all-gather.4.cloned.1.call-update) | async-done | bytes 1572880 | tf_op jit(solution)/shard_map/all_gather | solution.py:99
  141.7 0.0 copy-start.1
  141.7 2.6 fusion.15
  144.3 0.0 copy-done.2
  144.3 2.4 fusion.12
  146.7 212.0 %all-reduce.6 = (f32[96,12]{0,1:T(8,128)S(1)}, f32[96,12]{0,1:T(8,128)S(1)}) all-reduce(f32[96,12]{0,1:T(8,128)S(1)} %fusion.12, f32[96,12]{0,1:T(8,128)S(1)} %fusion.15), channel_id=1, replica_groups=mesh['slab'=64,'mode'=8] {'slab'}, use_global_device_ids=true, to_apply=%region_0.1 | all-reduce | flops 2304 | bytes 18432 | tf_op jit(solution)/shard_map/psum | solution.py:105
  358.7 34.3 %all-gather = f32[8,12,96]{2,1,0:T(8,128)S(1)} all-gather(f32[1,12,96]{2,1,0:T(8,128)S(1)} %bitcast.67), channel_id=1, replica_groups=mesh['slab'=64,'mode'=8] {'mode'}, dimensions={0}, use_global_device_ids=true | all-gather | bytes 41472 | tf_op jit(solution)/shard_map/all_gather | solution.py:107
  393.0 0.1 copy.15
  393.1 8.8 %cholesky.17 = f32[96,96]{1,0:T(8,128)S(1)} custom-call(f32[96,96]{1,0:T(8,128)S(1)} %fusion.82), custom_call_target="Cholesky" | custom-call | tf_op jit(solution)/shard_map/jit(cholesky)/cholesky | solution.py:69
  401.9 0.6 compare_reduce_fusion
  402.6 0.7 fusion.79
  403.2 7.4 %custom-call.7 = f32[1,96,96]{1,2,0:T(8,128)S(1)} custom-call(f32[1,96,96]{2,1,0:T(8,128)S(1)} %fusion.79), custom_call_target="InvertDiagBlocksLowerTriangular" | custom-call | tf_op jit(solution)/shard_map/jit(_solve_triangular)/triangular_solve | solution.py:70
  410.6 0.2 fusion.80
  410.8 34.2 %all-gather.1 = f32[8,12,96]{2,1,0:T(8,128)S(1)} all-gather(f32[1,12,96]{2,1,0:T(8,128)S(1)} %bitcast.66), channel_id=1, replica_groups=mesh['slab'=64,'mode'=8] {'mode'}, dimensions={0}, use_global_device_ids=true | all-gather | bytes 41472 | tf_op jit(solution)/shard_map/all_gather | solution.py:108
  445.0 0.2 fusion.90
  445.2 0.8 fusion.91
  446.1 0.0 copy-done.1
  446.1 1.0 fusion
  447.1 0.7 bitcast_bitcast_fusion
  (5 shorter events, 0.1 us)
Async XLA Ops:
  7.2 134.5 %all-gather.4.cloned.1.call-start = ((), (), s32[]{:S(2)}) async-start(), calls=%async_computation | async-start | bytes 1769472 | tf_op jit(solution)/shard_map/all_gather | solution.py:99
  8.0 15.0 %copy-start = (bf16[12,1,64,128]{3,2,1,0:T(8,128)(2,1)S(1)}, bf16[12,1,64,128]{3,2,1,0:T(8,128)(2,1)}, u32[]{:S(2)}) copy-start(bf16[12,1,64,128]{3,2,1,0:T(8,128)(2,1)} %param.4) | copy-start | bytes 589828
  9.0 13.2 %collective-permute-start.1 = (f32[12,1,64,128]{3,2,1,0:T(8,128)S(1)}, f32[12,1,64,128]{3,2,1,0:T(8,128)S(1)}, u32[]{:S(2)}, u32[]{:S(2)}) collective-permute-start(f32[12,1,64,128]{3,2,1,0:T(8,128)S(1)} %convert_multiply_fusion), channel_id=1, source_target_pairs={{0,8},{8,16},{16,24},{24,32},{32,40},{40,48},{48,56},{56,64},{64,7... | collective-permute-start | bytes 1179656 | tf_op jit(solution)/shard_map/ppermute | solution.py:18
  10.8 11.4 %collective-permute-start.3 = (f32[12,1,64,128]{3,2,1,0:T(8,128)S(1)}, f32[12,1,64,128]{3,2,1,0:T(8,128)S(1)}, u32[]{:S(2)}, u32[]{:S(2)}) collective-permute-start(f32[12,1,64,128]{3,2,1,0:T(8,128)S(1)} %convert_multiply_fusion), channel_id=1, source_target_pairs={{8,0},{16,8},{24,16},{32,24},{40,32},{48,40},{56,48},{64,56},{72,6... | collective-permute-start | bytes 1179656 | tf_op jit(solution)/shard_map/ppermute | solution.py:19
  12.9 6.6 %collective-permute-start = (f32[1,64,128]{2,1,0:T(8,128)S(1)}, f32[1,64,128]{2,1,0:T(8,128)S(1)}, u32[]{:S(2)}, u32[]{:S(2)}) collective-permute-start(f32[1,64,128]{2,1,0:T(8,128)S(1)} %select_add_fusion), channel_id=1, source_target_pairs={{0,8},{8,16},{16,24},{24,32},{32,40},{40,48},{48,56},{56,64},{64,7... | collective-permute-start | bytes 98312 | tf_op jit(solution)/shard_map/ppermute | solution.py:18
  16.9 4.3 collective-permute-start.2
  23.5 5.9 %collective-permute-start.4 = (f32[12,1,64,128]{3,2,1,0:T(8,128)S(1)}, f32[12,1,64,128]{3,2,1,0:T(8,128)S(1)}, u32[]{:S(2)}, u32[]{:S(2)}) collective-permute-start(f32[12,1,64,128]{3,2,1,0:T(8,128)S(1)} %fusion.66), channel_id=1, source_target_pairs={{0,8},{8,16},{16,24},{24,32},{32,40},{40,48},{48,56},{56,64},{64,7... | collective-permute-start | bytes 1179656 | tf_op jit(solution)/shard_map/ppermute | solution.py:18
  28.1 4.3 collective-permute-start.5
  33.7 10.3 %collective-permute-start.6 = (f32[12,1,64,128]{3,2,1,0:T(8,128)S(1)}, f32[12,1,64,128]{3,2,1,0:T(8,128)S(1)}, u32[]{:S(2)}, u32[]{:S(2)}) collective-permute-start(f32[12,1,64,128]{3,2,1,0:T(8,128)S(1)} %fusion.56), channel_id=1, source_target_pairs={{0,8},{8,16},{16,24},{24,32},{32,40},{40,48},{48,56},{56,64},{64,7... | collective-permute-start | bytes 1179656 | tf_op jit(solution)/shard_map/ppermute | solution.py:18
  42.7 3.6 collective-permute-start.7
  47.6 9.6 %collective-permute-start.8 = (f32[12,1,64,128]{3,2,1,0:T(8,128)S(1)}, f32[12,1,64,128]{3,2,1,0:T(8,128)S(1)}, u32[]{:S(2)}, u32[]{:S(2)}) collective-permute-start(f32[12,1,64,128]{3,2,1,0:T(8,128)S(1)} %fusion.44), channel_id=1, source_target_pairs={{0,8},{8,16},{16,24},{24,32},{32,40},{40,48},{48,56},{56,64},{64,7... | collective-permute-start | bytes 1179656 | tf_op jit(solution)/shard_map/ppermute | solution.py:18
  55.9 3.6 collective-permute-start.9
  61.5 9.6 %collective-permute-start.10 = (f32[12,1,64,128]{3,2,1,0:T(8,128)S(1)}, f32[12,1,64,128]{3,2,1,0:T(8,128)S(1)}, u32[]{:S(2)}, u32[]{:S(2)}) collective-permute-start(f32[12,1,64,128]{3,2,1,0:T(8,128)S(1)} %get-tuple-element.11), channel_id=1, source_target_pairs={{0,8},{8,16},{16,24},{24,32},{32,40},{40,48},{48,56},{56,64},{64,7... | collective-permute-start | bytes 1179656 | tf_op jit(solution)/shard_map/ppermute | solution.py:18
  69.8 3.6 collective-permute-start.11
  74.2 70.1 %copy-start.2 = (bf16[12,1,64,128]{3,2,1,0:T(8,128)(2,1)S(1)}, bf16[12,1,64,128]{3,2,1,0:T(8,128)(2,1)}, u32[]{:S(2)}) copy-start(bf16[12,1,64,128]{3,2,1,0:T(8,128)(2,1)} %get-tuple-element.10) | copy-start | bytes 589828
  141.7 304.4 %copy-start.1 = (bf16[96,1,64,128]{3,2,1,0:T(8,128)(2,1)S(1)}, bf16[96,1,64,128]{3,2,1,0:T(8,128)(2,1)}, u32[]{:S(2)}) copy-start(bf16[96,1,64,128]{3,2,1,0:T(8,128)(2,1)} %all-gather.4.cloned.1.call-done) | copy-start | bytes 4718596
Sparse Core Ops, SparseCore 0:
  61.6 80.0 all-gather.3
where the time goes:
time: 455 us
  blocking collectives  280 us (62%)
  waiting for transfers between devices  78.8 us (17%)
  starting transfers between devices  43.7 us (10%)
  other arithmetic  28 us (6%)
  between operations  15.6 us (3%)
  matrix products  7.25 us (2%)
    psum x1, blocking collectives, per_device(): gram_sum, cross_sum = lax.psum((gram_block, cross_block), 'slab')  212 us
    all_gather x1, waiting for transfers between devices, per_device(): everything = lax.all_gather(filtered, 'mode', axis=0, tiled=True)  67 us
    ppermute x6, starting transfers between devices, padded_2(): before = lax.ppermute(last, axis, up)  35.9 us
    all_gather x1, blocking collectives, per_device(): lax.all_gather(gram_sum, 'mode', axis=1, tiled=True)  34.3 us
    all_gather x1, blocking collectives, per_device(): lax.all_gather(cross_sum, 'mode', axis=1, tiled=True)  34.2 us
    ppermute x6, waiting for transfers between devices, padded_2(): after = lax.ppermute(first, axis, down)  11.7 us
    another operation x3, other arithmetic, factor(): lower = jnp.linalg.cholesky(gram)  9.45 us
  transfers between devices with their start and end apart: 13, of which 6 were waited for; matrix products, arithmetic and copies ran while one was open for 1% of the time, Pallas kernels for 0%

commit v1 on v0

--- a/solution.py
+++ b/solution.py
@@ -105,7 +105,9 @@
     gram_sum, cross_sum = lax.psum((gram_block, cross_block), "slab")
     gram, cross = (
         lax.all_gather(gram_sum, "mode", axis=1, tiled=True),
-        lax.all_gather(cross_sum, "mode", axis=1, tiled=True),
+        jnp.concatenate(
+            lax.all_to_all(jnp.stack([cross_sum] * lax.axis_size("mode")), "mode", 0, 0), axis=1
+        ),
     )
     projected, rotation = factor(gram, cross)
     columns = lax.dynamic_slice_in_dim(rotation, lax.axis_index("mode") * local, local, 1)

time: 455 us -> 432 us (0.949)
  the two profiles are of different devices: /device:TPU:4 before, /device:TPU:8 now
where the time goes in v1:
time: 432 us; the launch traced here: 431 us
  blocking collectives  243 us (56%)
  waiting for transfers between devices  85.2 us (20%)
  starting transfers between devices  50.9 us (12%)
  other arithmetic  28 us (6%)
  between operations  15.6 us (4%)
  matrix products  7.25 us (2%)
    psum x1, blocking collectives, per_device(): gram_sum, cross_sum = lax.psum((gram_block, cross_block), 'slab')  210 us
    all_gather x1, waiting for transfers between devices, per_device(): everything = lax.all_gather(filtered, 'mode', axis=0, tiled=True)  69.1 us
    ppermute x6, starting transfers between devices, padded_2(): before = lax.ppermute(last, axis, up)  36.2 us
    all_gather x1, blocking collectives, per_device(): lax.all_gather(gram_sum, 'mode', axis=1, tiled=True)  33.2 us
    ppermute x6, waiting for transfers between devices, padded_2(): after = lax.ppermute(first, axis, down)  11.4 us
    another operation x3, other arithmetic, factor(): lower = jnp.linalg.cholesky(gram)  9.45 us
  transfers between devices with their start and end apart: 14, of which 7 were waited for; matrix products, arithmetic and copies ran while one was open for 1% of the time, Pallas kernels for 0%

profile of v1, /device:TPU:8, one launch (start us, length us, event | category | flops | bytes accessed | tf_op | source)
XLA Modules:
  0.0 431.2 jit_solution(7965790386469745461)
XLA Ops:
  7.2 0.0 all-gather.3.cloned.1.call-start
  7.2 0.8 convert_bitcast_fusion
  8.0 0.0 copy-start
  8.0 1.0 convert_multiply_fusion
  9.0 1.8 collective-permute-start.1
  10.8 1.3 collective-permute-start.3
  12.1 0.8 select_add_fusion
  12.9 4.3 collective-permute-start
  17.1 1.3 collective-permute-start.2
  19.7 0.0 collective-permute-done
  19.8 1.7 collective-permute-done.2
  21.5 0.1 select_maximum_fusion.10
  21.6 0.9 multiply_bitcast_fusion.1
  22.5 0.0 collective-permute-done.1
  22.5 0.0 collective-permute-done.3
  22.5 0.8 select_maximum_fusion.8
  23.3 0.0 copy-done
  23.3 0.5 fusion.66
  23.8 4.6 %collective-permute-start.4 = (f32[12,1,64,128]{3,2,1,0:T(8,128)S(1)}, f32[12,1,64,128]{3,2,1,0:T(8,128)S(1)}, u32[]{:S(2)}, u32[]{:S(2)}) collective-permute-start(f32[12,1,64,128]{3,2,1,0:T(8,128)S(1)} %fusion.66), channel_id=1, source_target_pairs={{0,8},{8,16},{16,24},{24,32},{32,40},{40,48},{48,56},{56,64},{64,7... | collective-permute-start | bytes 1179656 | tf_op jit(solution)/shard_map/ppermute | solution.py:18
  28.3 1.3 collective-permute-start.5
  29.6 0.0 collective-permute-done.4
  29.7 2.7 collective-permute-done.5
  32.4 0.8 select_maximum_fusion.6
  33.2 0.5 fusion.56
  33.7 9.0 %collective-permute-start.6 = (f32[12,1,64,128]{3,2,1,0:T(8,128)S(1)}, f32[12,1,64,128]{3,2,1,0:T(8,128)S(1)}, u32[]{:S(2)}, u32[]{:S(2)}) collective-permute-start(f32[12,1,64,128]{3,2,1,0:T(8,128)S(1)} %fusion.56), channel_id=1, source_target_pairs={{0,8},{8,16},{16,24},{24,32},{32,40},{40,48},{48,56},{56,64},{64,7... | collective-permute-start | bytes 1179656 | tf_op jit(solution)/shard_map/ppermute | solution.py:18
  42.7 1.3 collective-permute-start.7
  44.0 0.0 collective-permute-done.6
  44.0 2.3 collective-permute-done.7
  46.3 0.8 select_maximum_fusion.4
  47.1 0.5 fusion.44
  47.6 8.3 %collective-permute-start.8 = (f32[12,1,64,128]{3,2,1,0:T(8,128)S(1)}, f32[12,1,64,128]{3,2,1,0:T(8,128)S(1)}, u32[]{:S(2)}, u32[]{:S(2)}) collective-permute-start(f32[12,1,64,128]{3,2,1,0:T(8,128)S(1)} %fusion.44), channel_id=1, source_target_pairs={{0,8},{8,16},{16,24},{24,32},{32,40},{40,48},{48,56},{56,64},{64,7... | collective-permute-start | bytes 1179656 | tf_op jit(solution)/shard_map/ppermute | solution.py:18
  55.9 1.3 collective-permute-start.9
  57.2 0.0 collective-permute-done.8
  57.2 2.3 collective-permute-done.9
  59.5 0.8 select_maximum_fusion.2
  60.3 1.2 fusion.88
  61.5 0.0 all-gather.3.cloned.1.call-update
  61.5 8.3 %collective-permute-start.10 = (f32[12,1,64,128]{3,2,1,0:T(8,128)S(1)}, f32[12,1,64,128]{3,2,1,0:T(8,128)S(1)}, u32[]{:S(2)}, u32[]{:S(2)}) collective-permute-start(f32[12,1,64,128]{3,2,1,0:T(8,128)S(1)} %get-tuple-element.11), channel_id=1, source_target_pairs={{0,8},{8,16},{16,24},{24,32},{32,40},{40,48},{48,56},{56,64},{64,7... | collective-permute-start | bytes 1179656 | tf_op jit(solution)/shard_map/ppermute | solution.py:18
  69.8 1.3 collective-permute-start.11
  71.1 0.0 collective-permute-done.10
  71.1 2.3 collective-permute-done.11
  73.4 0.8 select_maximum_fusion
  74.2 0.0 copy-start.2
  74.2 0.5 fusion.78
  74.7 69.1 %all-gather.3.cloned.1.call-done = bf16[96,1,64,128]{3,2,1,0:T(8,128)(2,1)} async-done(((bf16[12,1,64,128]{3,2,1,0:T(8,128)(2,1)}), bf16[96,1,64,128]{3,2,1,0:T(8,128)(2,1)}) %all-gather.3.cloned.1.call-update) | async-done | bytes 1572880 | tf_op jit(solution)/shard_map/all_gather | solution.py:99
  143.8 2.6 fusion.15
  146.3 0.0 copy-done.2
  146.3 2.4 fusion.12
  148.8 209.5 %all-reduce.6 = (f32[96,12]{0,1:T(8,128)S(1)}, f32[96,12]{0,1:T(8,128)S(1)}) all-reduce(f32[96,12]{0,1:T(8,128)S(1)} %fusion.12, f32[96,12]{0,1:T(8,128)S(1)} %fusion.15), channel_id=1, replica_groups=mesh['slab'=64,'mode'=8] {'slab'}, use_global_device_ids=true, to_apply=%region_0.1 | all-reduce | flops 2304 | bytes 18432 | tf_op jit(solution)/shard_map/psum | solution.py:105
  358.3 33.2 %all-gather = f32[8,12,96]{2,1,0:T(8,128)S(1)} all-gather(f32[1,12,96]{2,1,0:T(8,128)S(1)} %bitcast.67), channel_id=1, replica_groups=mesh['slab'=64,'mode'=8] {'mode'}, dimensions={0}, use_global_device_ids=true | all-gather | bytes 41472 | tf_op jit(solution)/shard_map/all_gather | solution.py:107
  391.5 0.1 copy.16
  391.6 8.8 %cholesky.17 = f32[96,96]{1,0:T(8,128)S(1)} custom-call(f32[96,96]{1,0:T(8,128)S(1)} %fusion.82), custom_call_target="Cholesky" | custom-call | tf_op jit(solution)/shard_map/jit(cholesky)/cholesky | solution.py:69
  400.4 0.6 compare_reduce_fusion
  401.0 0.7 fusion.79
  401.7 7.4 %custom-call.7 = f32[1,96,96]{1,2,0:T(8,128)S(1)} custom-call(f32[1,96,96]{2,1,0:T(8,128)S(1)} %fusion.79), custom_call_target="InvertDiagBlocksLowerTriangular" | custom-call | tf_op jit(solution)/shard_map/jit(_solve_triangular)/triangular_solve | solution.py:70
  409.0 0.2 fusion.80
  409.3 0.6 stack.2
  409.9 6.9 %all-to-all-start = ((f32[8,96,12]{1,2,0:T(8,128)}), f32[8,96,12]{1,2,0:T(8,128)S(1)}, u32[]{:S(2)}, u32[]{:S(2)}) async-start(f32[8,96,12]{1,2,0:T(8,128)} %stack.2), calls=%async_computation | async-start | bytes 131072 | tf_op jit(solution)/shard_map/all_to_all | solution.py:109
  416.8 0.0 copy-done.1
  416.8 1.0 fusion
  417.8 0.7 bitcast_bitcast_fusion
  418.5 4.7 %all-to-all-done = f32[8,96,12]{1,2,0:T(8,128)S(1)} async-done(((f32[8,96,12]{1,2,0:T(8,128)}), f32[8,96,12]{1,2,0:T(8,128)S(1)}, u32[]{:S(2)}, u32[]{:S(2)}) %all-to-all-start) | async-done | bytes 36896 | tf_op jit(solution)/shard_map/all_to_all | solution.py:109
  423.2 0.2 fusion.90
  423.5 0.8 fusion.91
  (6 shorter events, 0.1 us)
Async XLA Ops:
  7.2 136.6 %all-gather.3.cloned.1.call-start = ((), (), s32[]{:S(2)}) async-start(), calls=%async_computation.1 | async-start | bytes 1769472 | tf_op jit(solution)/shard_map/all_gather | solution.py:99
  8.0 15.3 %copy-start = (bf16[12,1,64,128]{3,2,1,0:T(8,128)(2,1)S(1)}, bf16[12,1,64,128]{3,2,1,0:T(8,128)(2,1)}, u32[]{:S(2)}) copy-start(bf16[12,1,64,128]{3,2,1,0:T(8,128)(2,1)} %param.4) | copy-start | bytes 589828
  9.0 13.5 %collective-permute-start.1 = (f32[12,1,64,128]{3,2,1,0:T(8,128)S(1)}, f32[12,1,64,128]{3,2,1,0:T(8,128)S(1)}, u32[]{:S(2)}, u32[]{:S(2)}) collective-permute-start(f32[12,1,64,128]{3,2,1,0:T(8,128)S(1)} %convert_multiply_fusion), channel_id=1, source_target_pairs={{0,8},{8,16},{16,24},{24,32},{32,40},{40,48},{48,56},{56,64},{64,7... | collective-permute-start | bytes 1179656 | tf_op jit(solution)/shard_map/ppermute | solution.py:18
  10.8 11.7 %collective-permute-start.3 = (f32[12,1,64,128]{3,2,1,0:T(8,128)S(1)}, f32[12,1,64,128]{3,2,1,0:T(8,128)S(1)}, u32[]{:S(2)}, u32[]{:S(2)}) collective-permute-start(f32[12,1,64,128]{3,2,1,0:T(8,128)S(1)} %convert_multiply_fusion), channel_id=1, source_target_pairs={{8,0},{16,8},{24,16},{32,24},{40,32},{48,40},{56,48},{64,56},{72,6... | collective-permute-start | bytes 1179656 | tf_op jit(solution)/shard_map/ppermute | solution.py:19
  12.9 6.9 %collective-permute-start = (f32[1,64,128]{2,1,0:T(8,128)S(1)}, f32[1,64,128]{2,1,0:T(8,128)S(1)}, u32[]{:S(2)}, u32[]{:S(2)}) collective-permute-start(f32[1,64,128]{2,1,0:T(8,128)S(1)} %select_add_fusion), channel_id=1, source_target_pairs={{0,8},{8,16},{16,24},{24,32},{32,40},{40,48},{48,56},{56,64},{64,7... | collective-permute-start | bytes 98312 | tf_op jit(solution)/shard_map/ppermute | solution.py:18
  17.1 4.3 %collective-permute-start.2 = (f32[1,64,128]{2,1,0:T(8,128)S(1)}, f32[1,64,128]{2,1,0:T(8,128)S(1)}, u32[]{:S(2)}, u32[]{:S(2)}) collective-permute-start(f32[1,64,128]{2,1,0:T(8,128)S(1)} %select_add_fusion), channel_id=1, source_target_pairs={{8,0},{16,8},{24,16},{32,24},{40,32},{48,40},{56,48},{64,56},{72,6... | collective-permute-start | bytes 98312 | tf_op jit(solution)/shard_map/ppermute | solution.py:19
  23.8 5.9 %collective-permute-start.4 = (f32[12,1,64,128]{3,2,1,0:T(8,128)S(1)}, f32[12,1,64,128]{3,2,1,0:T(8,128)S(1)}, u32[]{:S(2)}, u32[]{:S(2)}) collective-permute-start(f32[12,1,64,128]{3,2,1,0:T(8,128)S(1)} %fusion.66), channel_id=1, source_target_pairs={{0,8},{8,16},{16,24},{24,32},{32,40},{40,48},{48,56},{56,64},{64,7... | collective-permute-start | bytes 1179656 | tf_op jit(solution)/shard_map/ppermute | solution.py:18
  28.3 4.0 collective-permute-start.5
  33.7 10.3 %collective-permute-start.6 = (f32[12,1,64,128]{3,2,1,0:T(8,128)S(1)}, f32[12,1,64,128]{3,2,1,0:T(8,128)S(1)}, u32[]{:S(2)}, u32[]{:S(2)}) collective-permute-start(f32[12,1,64,128]{3,2,1,0:T(8,128)S(1)} %fusion.56), channel_id=1, source_target_pairs={{0,8},{8,16},{16,24},{24,32},{32,40},{40,48},{48,56},{56,64},{64,7... | collective-permute-start | bytes 1179656 | tf_op jit(solution)/shard_map/ppermute | solution.py:18
  42.7 3.6 collective-permute-start.7
  47.6 9.6 %collective-permute-start.8 = (f32[12,1,64,128]{3,2,1,0:T(8,128)S(1)}, f32[12,1,64,128]{3,2,1,0:T(8,128)S(1)}, u32[]{:S(2)}, u32[]{:S(2)}) collective-permute-start(f32[12,1,64,128]{3,2,1,0:T(8,128)S(1)} %fusion.44), channel_id=1, source_target_pairs={{0,8},{8,16},{16,24},{24,32},{32,40},{40,48},{48,56},{56,64},{64,7... | collective-permute-start | bytes 1179656 | tf_op jit(solution)/shard_map/ppermute | solution.py:18
  55.9 3.6 collective-permute-start.9
  61.5 9.6 %collective-permute-start.10 = (f32[12,1,64,128]{3,2,1,0:T(8,128)S(1)}, f32[12,1,64,128]{3,2,1,0:T(8,128)S(1)}, u32[]{:S(2)}, u32[]{:S(2)}) collective-permute-start(f32[12,1,64,128]{3,2,1,0:T(8,128)S(1)} %get-tuple-element.11), channel_id=1, source_target_pairs={{0,8},{8,16},{16,24},{24,32},{32,40},{40,48},{48,56},{56,64},{64,7... | collective-permute-start | bytes 1179656 | tf_op jit(solution)/shard_map/ppermute | solution.py:18
  69.8 3.6 collective-permute-start.11
  74.2 72.2 %copy-start.2 = (bf16[12,1,64,128]{3,2,1,0:T(8,128)(2,1)S(1)}, bf16[12,1,64,128]{3,2,1,0:T(8,128)(2,1)}, u32[]{:S(2)}) copy-start(bf16[12,1,64,128]{3,2,1,0:T(8,128)(2,1)} %get-tuple-element.10) | copy-start | bytes 589828
  143.8 273.1 %copy-start.1 = (bf16[96,1,64,128]{3,2,1,0:T(8,128)(2,1)S(1)}, bf16[96,1,64,128]{3,2,1,0:T(8,128)(2,1)}, u32[]{:S(2)}) copy-start(bf16[96,1,64,128]{3,2,1,0:T(8,128)(2,1)} %all-gather.3.cloned.1.call-done) | copy-start | bytes 4718596
  409.9 13.3 %all-to-all-start = ((f32[8,96,12]{1,2,0:T(8,128)}), f32[8,96,12]{1,2,0:T(8,128)S(1)}, u32[]{:S(2)}, u32[]{:S(2)}) async-start(f32[8,96,12]{1,2,0:T(8,128)} %stack.2), calls=%async_computation | async-start | bytes 131072 | tf_op jit(solution)/shard_map/all_to_all | solution.py:109
Sparse Core Ops, SparseCore 0:
  61.6 82.1 all-gather.2
